TPU v7x, 32 devices: a whole 2x2x4 slice. The times are simulated.
32 devices in a mesh: groups: 2 (over y), clusters: 16 (over z, x, core).
Axes of the slice: x: 2, y: 2, z: 4, core: 2. Of those that a mesh axis runs over, the one named last changes fastest.
Arguments:
- right_side: float32 [64, 512, 128], P(('groups', 'clusters')), parts along dimension 0, may hold values from -6 to 6
- diag_shift: float32 [64, 512], P(('groups', 'clusters')), parts along dimension 0, may hold values from 10 to 20
- self_blocks: bfloat16 [64, 512, 512], P(('groups', 'clusters')), parts along dimension 0, may hold values from -0.049804688 to 0.049804688
- near_blocks: bfloat16 [64, 512, 2048], P(('groups', 'clusters')), parts along dimension 0, may hold values from -0.019897461 to 0.019897461
- near_offset: int32 [256], P(('groups', 'clusters')), parts along dimension 0, may hold values from -2 to 2
- near_column: int32 [256], P(('groups', 'clusters')), parts along dimension 0, may hold values from 0 to 1
- far_factors: bfloat16 [64, 512, 2048], P(('groups', 'clusters')), parts along dimension 0, may hold values from -0.049804688 to 0.049804688
- far_peer: int32 [4096, 1], P(('groups', 'clusters')), parts along dimension 0, may hold values from 0 to 15; in each aligned block of 128 rows (0 to 127, 128 to 255, ...) at most 8 rows name the same one
Outputs:
- solution_field: float32 [64, 512, 128], P(('groups', 'clusters')), parts along dimension 0
- residual: float32 [64, 512, 128], P(('groups', 'clusters')), parts along dimension 0
There are 2 independent parts, one for each index of `groups`. A program takes and returns all parts, laid end to end along the dimension named above; each array names one. Nothing has to cross between parts.
Inputs may be any that keep to these rules, and one draw needn't show every extreme that they name: `far_peer`: in the rows of one device no device is named more than 8 times, and some device is named exactly 8 times in some device's rows.
All inputs are finite; a program needn't handle non-finite values.
Results may differ from a plain program's by a relative error of at most 0.0003.
Values may be sent and summed in bfloat16 or wider, within the bound.
A program may use at most 128 MiB of HBM per device.

v0:
```python
import functools

import jax
import jax.numpy as jnp
from jax import lax
from jax.experimental import pallas as pl
from jax.experimental.pallas import tpu as pltpu
from jax.sharding import PartitionSpec as P

MESH = pl.DeviceIdType.MESH
RANK = 32
REACH = 2
ITERS = 2
HIGH = lax.Precision.HIGHEST


def hdot(left, right, dims=((1,), (0,))):
    return lax.dot_general(left, right, (dims, ((), ())), precision=HIGH, preferred_element_type=jnp.float32)


def invert(mats):
    size = mats[0].shape[0]
    rows = lax.broadcasted_iota(jnp.int32, (size, size), 0)
    lanes = lax.broadcasted_iota(jnp.int32, (size, size), 1)

    def body(_, mats):
        done = []
        for a in mats:
            for k in range(8):
                column = a[:, k : k + 1]
                pivot = 1.0 / a[k : k + 1, k : k + 1]
                line = jnp.where(lanes[:1] == k, pivot, a[k : k + 1] * pivot)
                a = jnp.where(rows == k, line, jnp.where(lanes == k, 0.0, a) - column * line)
            a = pltpu.roll(a, size - 8, 1)
            done.append(jnp.concatenate([a[8:], a[:8]], axis=0))
        return tuple(done)

    return lax.fori_loop(0, size // 8, body, tuple(mats))


def meet(devices):
    me = lax.axis_index("clusters")
    barrier = pltpu.get_barrier_semaphore()

    def greet(k, carry):
        peer = lax.rem(me + k, devices)
        pl.semaphore_signal(barrier, inc=1, device_id={"clusters": peer}, device_id_type=MESH)
        return carry

    lax.fori_loop(1, devices, greet, 0)
    pl.semaphore_wait(barrier, devices - 1)


def reduce_all(devices, part, landing, total, sems):
    me = lax.axis_index("clusters")
    pieces = part.shape[0]
    send_a, recv_a, send_b, recv_b = sems

    def copy_a(k, peer):
        return pltpu.make_async_remote_copy(
            src_ref=part.at[peer], dst_ref=landing.at[k], send_sem=send_a.at[k], recv_sem=recv_a.at[k],
            device_id={"clusters": peer}, device_id_type=MESH)

    def copy_b(k, peer, piece):
        return pltpu.make_async_remote_copy(
            src_ref=total.at[piece], dst_ref=total.at[piece], send_sem=send_b.at[k], recv_sem=recv_b.at[k],
            device_id={"clusters": peer}, device_id_type=MESH)

    def loop(fn):
        def body(k, carry):
            fn(k)
            return carry
        lax.fori_loop(1, devices, body, 0)

    def send_one(k):
        peer = lax.rem(me + k, devices)
        if pieces == devices:
            copy_a(k, peer).start()
        else:
            @pl.when(peer < pieces)
            def _():
                copy_a(k, peer).start()

    loop(send_one)

    def gather():
        def add(k, acc):
            copy_a(k, 0).wait_recv()
            return acc + landing[k]
        total[me] = lax.fori_loop(1, devices, add, part[me])
        loop(lambda k: copy_b(k, lax.rem(me + k, devices), me).start())

    if pieces == devices:
        gather()
    else:
        pl.when(me < pieces)(gather)

    def arrive(k):
        origin = lax.rem(me - k + devices, devices)
        if pieces == devices:
            copy_b(k, 0, origin).wait_recv()
        else:
            @pl.when(origin < pieces)
            def _():
                copy_b(k, 0, origin).wait_recv()

    loop(arrive)

    def finish(k):
        peer = lax.rem(me + k, devices)
        if pieces == devices:
            copy_a(k, peer).wait_send()
            copy_b(k, peer, me).wait_send()
        else:
            @pl.when(peer < pieces)
            def _():
                copy_a(k, peer).wait_send()

            @pl.when(me < pieces)
            def _():
                copy_b(k, peer, me).wait_send()

    loop(finish)


def symmetric(mat):
    return 0.5 * (mat + mat.T)


def first_kernel(devices, part, step_ref, later_ref, blend_ref, landing, total, *sems):
    meet(devices)
    reduce_all(devices, part, landing, total, sems)
    modes = part.shape[-1]
    whole = total[...].reshape(-1, modes)
    current, curvature, squared = whole[:modes], whole[modes : 2 * modes], whole[2 * modes :]
    inv_curv, inv_cur = invert([symmetric(curvature), symmetric(current)])
    step = hdot(inv_curv, current)
    cross = hdot(curvature, step)
    later = current - cross - cross.T + hdot(step.T, hdot(squared, step))
    step_ref[...] = step
    later_ref[...] = later
    blend_ref[...] = hdot(inv_cur, later)


def last_kernel(devices, part, current, step_ref, landing, total, *sems):
    meet(devices)
    reduce_all(devices, part, landing, total, sems)
    (inv_curv,) = invert([symmetric(total[...].reshape(part.shape[-1], part.shape[-1]))])
    step_ref[...] = hdot(inv_curv, current[...])


def solve_call(kernel, grams, extra, outs, ident):
    devices = lax.axis_size("clusters")
    modes = grams.shape[-1]
    pieces = min(devices, grams.shape[0] // 8)
    part = grams.reshape(pieces, -1, modes)
    square = jax.ShapeDtypeStruct((modes, modes), jnp.float32)
    vmem = pl.BlockSpec(memory_space=pltpu.VMEM)
    return pl.pallas_call(
        functools.partial(kernel, devices),
        out_shape=[square] * outs,
        in_specs=[vmem] * (1 + len(extra)),
        out_specs=[vmem] * outs,
        scratch_shapes=[
            pltpu.VMEM((devices,) + part.shape[1:], jnp.float32),
            pltpu.VMEM(part.shape, jnp.float32),
        ] + [pltpu.SemaphoreType.DMA((devices,))] * 4,
        compiler_params=pltpu.CompilerParams(collective_id=ident, has_side_effects=True, vmem_limit_bytes=32 << 20),
    )(part, *extra)


def from_behind(value, axis, steps):
    count = lax.axis_size(axis)
    leading, last = (max(0, -steps), min(count, count - steps))
    return lax.ppermute(value, axis, [(source, source + steps) for source in range(leading, last)])


def local_gram(left, right):
    modes = left.shape[-1]
    return jnp.dot(
        left.reshape(-1, modes).T, right.reshape(-1, modes), precision=lax.Precision.HIGHEST
    )


def combine(block, coeff):
    modes = block.shape[-1]
    return jnp.dot(block.reshape(-1, modes), coeff, precision=lax.Precision.HIGHEST).reshape(
        block.shape
    )


def shards(
    right_side,
    diag_shift,
    self_blocks,
    near_blocks,
    near_offset,
    near_column,
    far_factors,
    far_peer,
):
    cl_dev, panels, modes = right_side.shape
    devices = lax.axis_size("clusters")
    far_dev = far_peer.shape[0]
    near_cl = near_blocks.shape[2] // panels
    capacity = max(2, -(-far_dev // devices))
    peers = far_peer[:, 0]
    peer_hot = (peers[:, None] == jnp.arange(devices, dtype=jnp.int32)[None, :]).astype(jnp.int32)
    earlier = jnp.cumsum(peer_hot, axis=0) - peer_hot
    ranking = jnp.sum(earlier * peer_hot, axis=1)
    slot_of = peers * capacity + ranking
    slot_table = (
        slot_of[None, :] == jnp.arange(devices * capacity, dtype=jnp.int32)[:, None]
    ).astype(jnp.bfloat16)
    span = 2 * REACH + 1
    window_pos = (near_offset + REACH) * cl_dev + near_column
    window_table = (
        window_pos[None, :] == jnp.arange(span * cl_dev, dtype=jnp.int32)[:, None]
    ).astype(jnp.float32)
    residual = right_side
    direction = right_side
    for step in range(ITERS):
        packed = direction.astype(jnp.bfloat16)
        image = diag_shift[:, :, None] * direction
        straight = jnp.einsum(
            "cpk,ckm->cpm", self_blocks, packed, preferred_element_type=jnp.float32
        )
        flipped = jnp.einsum(
            "ckp,ckm->cpm", self_blocks, packed, preferred_element_type=jnp.float32
        )
        image = image + 0.5 * (straight + flipped)
        slabs = []
        for offset in range(-REACH, REACH + 1):
            if offset == 0:
                slabs.append(packed)
            else:
                slabs.append(from_behind(packed, "clusters", -offset))
        window = jnp.concatenate(slabs, axis=0)
        fetched = jnp.take(window, window_pos, axis=0).reshape(cl_dev, near_cl * panels, modes)
        image = image + jnp.einsum(
            "cpk,ckm->cpm", near_blocks, fetched, preferred_element_type=jnp.float32
        )
        mirrored = jnp.einsum(
            "cpk,cpm->ckm", near_blocks, packed, preferred_element_type=jnp.float32
        )
        mirrored = mirrored.reshape(cl_dev * near_cl, panels * modes)
        returned = jnp.dot(window_table, mirrored, precision=lax.Precision.HIGHEST).reshape(
            span, cl_dev, panels, modes
        )
        image = image + returned[REACH]
        for offset in range(-REACH, REACH + 1):
            if offset != 0:
                image = image + from_behind(returned[offset + REACH], "clusters", offset)
        compressed = jnp.einsum(
            "cpk,cpm->ckm", far_factors, packed, preferred_element_type=jnp.float32
        ).astype(jnp.bfloat16)
        compressed = compressed.reshape(far_dev, RANK * modes)
        outgoing = jnp.dot(slot_table, compressed, preferred_element_type=jnp.float32).astype(
            jnp.bfloat16
        )
        outgoing = outgoing.reshape(devices, capacity, RANK * modes)
        incoming = lax.all_to_all(
            outgoing, "clusters", split_axis=0, concat_axis=0, tiled=True
        ).reshape(devices * capacity, RANK * modes)
        matched = jnp.dot(slot_table.T, incoming, preferred_element_type=jnp.float32).astype(
            jnp.bfloat16
        )
        matched = matched.reshape(cl_dev, far_dev // cl_dev * RANK, modes)
        image = image + jnp.einsum(
            "cpk,ckm->cpm", far_factors, matched, preferred_element_type=jnp.float32
        )
        if step == 0:
            grams = jnp.concatenate(
                [local_gram(residual, residual), local_gram(direction, image), local_gram(image, image)]
            )
            step_size, current, blend = solve_call(first_kernel, grams, (), 3, 1)
            solution_field = combine(direction, step_size)
            residual = residual - combine(image, step_size)
            direction = residual + combine(direction, blend)
        else:
            (step_size,) = solve_call(last_kernel, local_gram(direction, image), (current,), 1, 2)
            solution_field = solution_field + combine(direction, step_size)
            residual = residual - combine(image, step_size)
    return (solution_field, residual)


def solution(mesh):
    in_specs = (
        P(("groups", "clusters"), None, None),
        P(("groups", "clusters"), None),
        P(("groups", "clusters"), None, None),
        P(("groups", "clusters"), None, None),
        P(("groups", "clusters")),
        P(("groups", "clusters")),
        P(("groups", "clusters"), None, None),
        P(("groups", "clusters"), None),
    )
    out_specs = (P(("groups", "clusters"), None, None), P(("groups", "clusters"), None, None))
    return jax.shard_map(shards, mesh=mesh, in_specs=in_specs, out_specs=out_specs, check_vma=False)
```

profile of v0, /device:TPU:0, one launch (start us, length us, event | category | flops | bytes accessed | tf_op | source)
XLA Modules:
  0.0 256.8 jit_solution(4657958919736184775)
XLA Ops:
  1.8 5.5 %collective-permute-start = (bf16[2,512,128]{2,1,0:T(8,128)(2,1)S(1)}, bf16[2,512,128]{2,1,0:T(8,128)(2,1)}, u32[]{:S(2)}, u32[]{:S(2)}) collective-permute-start(bf16[2,512,128]{2,1,0:T(8,128)(2,1)S(1)} %convert_element_type.32), channel_id=1, source_target_pairs={{0,2},{1,3},{2,4},{3,5},{4,6},{5,7},{6,8},{7,9},{8,10},{9,11},{10,... | collective-permute-start | bytes 786440 | tf_op jit(solution)/shard_map/ppermute | solution.py:175
  12.1 4.9 %convolution_convert_fusion.5 = bf16[2,2048,128]{2,1,0:T(8,128)(2,1)} fusion(bf16[2,512,2048]{2,1,0:T(8,128)(2,1)} %param.16, bf16[2,512,128]{2,1,0:T(8,128)(2,1)S(1)} %convert_element_type.32), kind=kOutput, calls=%fused_computation.10 | convolution fusion | flops 537395200 | bytes 5505024 | tf_op jit(solution)/shard_map/cpk,cpm->ckm/dot_general | solution.py:254
  20.5 10.1 %all-to-all-start = ((bf16[16,8,4096]{2,1,0:T(8,128)(2,1)}), bf16[16,8,4096]{2,1,0:T(8,128)(2,1)}, u32[]{:S(2)}, u32[]{:S(2)}) async-start(bf16[16,8,4096]{2,1,0:T(8,128)(2,1)} %fusion), calls=%async_computation | async-start | bytes 2097152 | tf_op jit(solution)/shard_map/all_to_all | solution.py:262
  30.6 5.3 %fusion.40 = f32[2,2048,128]{2,1,0:T(8,128)} fusion(bf16[2,512,2048]{2,1,0:T(8,128)(2,1)} %param.13, bf16[2,512,128]{2,1,0:T(8,128)(2,1)S(1)} %convert_element_type.32), kind=kOutput, calls=%fused_computation.103 | convolution fusion | flops 536870912 | bytes 6553600 | tf_op jit(solution)/shard_map/cpk,cpm->ckm/dot_general | solution.py:243
  35.9 3.3 %reshape.117 = f32[8,65536]{1,0:T(8,128)} reshape(f32[2,2048,128]{2,1,0:T(8,128)} %fusion.40) | data formatting | bytes 4194304 | tf_op jit(solution)/shard_map/reshape | solution.py:246
  39.2 3.4 %fusion.35 = f32[10,65536]{1,0:T(8,128)S(1)} fusion(f32[8,65536]{1,0:T(8,128)} %reshape.117, s32[8]{0:T(128)S(1)} %get-tuple-element.12), kind=kOutput, calls=%fused_computation.93 | convolution fusion | flops 62914640 | bytes 4718624 | tf_op jit(solution)/shard_map/dot_general | solution.py:247
  53.4 3.8 %collective-permute-start.6 = (f32[2,512,128]{2,1,0:T(8,128)}, f32[2,512,128]{2,1,0:T(8,128)}, u32[]{:S(2)}, u32[]{:S(2)}) collective-permute-start(f32[2,512,128]{2,1,0:T(8,128)} %bitcast.166), channel_id=1, source_target_pairs={{0,1},{1,2},{2,3},{3,4},{4,5},{5,6},{6,7},{7,8},{8,9},{9,10},{10,1... | collective-permute-start | bytes 1572872 | tf_op jit(solution)/shard_map/ppermute | solution.py:175
  59.6 4.5 %collective-permute-start.7 = (f32[2,512,128]{2,1,0:T(8,128)}, f32[2,512,128]{2,1,0:T(8,128)}, u32[]{:S(2)}, u32[]{:S(2)}) collective-permute-start(f32[2,512,128]{2,1,0:T(8,128)} %bitcast.165), channel_id=1, source_target_pairs={{0,2},{1,3},{2,4},{3,5},{4,6},{5,7},{6,8},{7,9},{8,10},{9,11},{10,... | collective-permute-start | bytes 1572872 | tf_op jit(solution)/shard_map/ppermute | solution.py:175
  69.8 4.3 %convolution_bitcast_fusion.6 = f32[2,512,128]{2,1,0:T(8,128)} fusion(bf16[2,512,2048]{2,1,0:T(8,128)(2,1)} %param.13, bf16[2,2048,128]{2,1,0:T(8,128)(2,1)S(1)} %bitcast.175), kind=kOutput, calls=%fused_computation.38 | convolution fusion | flops 536870912 | bytes 5767168 | tf_op jit(solution)/shard_map/cpk,ckm->cpm/dot_general | solution.py:240
  77.1 3.8 %convolution_bitcast_fusion.5 = f32[2,512,128]{2,1,0:T(8,128)S(1)} fusion(bf16[2,512,2048]{2,1,0:T(8,128)(2,1)} %param.16, bf16[2,2048,128]{2,1,0:T(8,128)(2,1)} %reshape.121), kind=kOutput, calls=%fused_computation.37 | convolution fusion | flops 536870912 | bytes 5767168 | tf_op jit(solution)/shard_map/cpk,ckm->cpm/dot_general | solution.py:269
  81.0 2.3 fusion.21
  85.3 37.0 %shard_map.95 = (f32[128,128]{1,0:T(8,128)S(1)}, f32[128,128]{1,0:T(8,128)S(1)}, f32[128,128]{1,0:T(8,128)S(1)}) custom-call(f32[16,24,128]{2,1,0:T(8,128)S(1)} %bitcast.169), custom_call_target="tpu_custom_call" | custom-call | tf_op jit(solution)/shard_map/pallas_call | solution.py:159
  124.5 4.5 %collective-permute-start.8 = (bf16[2,512,128]{2,1,0:T(8,128)(2,1)S(1)}, bf16[2,512,128]{2,1,0:T(8,128)(2,1)}, u32[]{:S(2)}, u32[]{:S(2)}) collective-permute-start(bf16[2,512,128]{2,1,0:T(8,128)(2,1)S(1)} %get-tuple-element.9), channel_id=1, source_target_pairs={{0,2},{1,3},{2,4},{3,5},{4,6},{5,7},{6,8},{7,9},{8,10},{9,11},{10,... | collective-permute-start | bytes 786440 | tf_op jit(solution)/shard_map/ppermute | solution.py:175
  129.0 2.5 collective-permute-start.9
  134.3 4.3 %convolution_bitcast_fusion = f32[2,2048,128]{1,2,0:T(8,128)} fusion(bf16[2,512,128]{2,1,0:T(8,128)(2,1)S(1)} %get-tuple-element.9, bf16[2,512,2048]{2,1,0:T(8,128)(2,1)} %param.13), kind=kOutput, calls=%fused_computation.8 | convolution fusion | flops 536870912 | bytes 6553600 | tf_op jit(solution)/shard_map/cpk,cpm->ckm/dot_general | solution.py:243
  140.4 2.9 %copy.52 = f32[2,2048,128]{2,1,0:T(8,128)} copy(f32[2,2048,128]{1,2,0:T(8,128)} %convolution_bitcast_fusion) | data formatting | bytes 4194304 | tf_op jit(solution)/shard_map/cpk,cpm->ckm/dot_general | solution.py:243
  143.3 3.4 %reshape.128 = f32[8,65536]{1,0:T(8,128)} reshape(f32[2,2048,128]{2,1,0:T(8,128)} %copy.52) | data formatting | bytes 4194304 | tf_op jit(solution)/shard_map/reshape | solution.py:246
  146.6 5.3 %fusion.34 = f32[10,65536]{1,0:T(8,128)} fusion(f32[8,65536]{1,0:T(8,128)} %reshape.128, s32[8]{0:T(128)S(1)} %copy-done.13), kind=kOutput, calls=%fused_computation.92 | convolution fusion | flops 62914640 | bytes 4718624 | tf_op jit(solution)/shard_map/dot_general | solution.py:247
  151.9 2.3 copy.54
  154.2 2.3 reshape.129
  156.5 2.7 %fusion.1 = bf16[16,8,4096]{2,1,0:T(8,128)(2,1)} fusion(bf16[128,4096]{1,0:T(8,128)(2,1)} %reshape.129, s32[128]{0:T(128)S(1)} %multiply_add_fusion), kind=kOutput, calls=%fused_computation.7 | convolution fusion | flops 134758400 | bytes 2097664 | tf_op jit(solution)/shard_map/dot_general | solution.py:258
  159.2 9.3 %all-to-all-start.1 = ((bf16[16,8,4096]{2,1,0:T(8,128)(2,1)}), bf16[16,8,4096]{2,1,0:T(8,128)(2,1)}, u32[]{:S(2)}, u32[]{:S(2)}) async-start(bf16[16,8,4096]{2,1,0:T(8,128)(2,1)} %fusion.1), calls=%async_computation.1 | async-start | bytes 2097152 | tf_op jit(solution)/shard_map/all_to_all | solution.py:262
  168.4 5.9 %slice_bitcast_fusion.4 = (f32[1,2,512,128]{3,1,2,0:T(2,128)}, f32[1,2,512,128]{3,1,2,0:T(2,128)S(1)}, f32[1,2,512,128]{3,1,2,0:T(2,128)S(1)}, f32[1,2,512,128]{3,1,2,0:T(2,128)S(1)}, f32[1,2,512,128]{3,1,2,0:T(2,128)S(1)}) fusion(f32[10,65536]{1,0:T(8,128)} %fusion.34), kind=kLoop, calls=%fused_computation.61 | loop fusion | bytes 5242880
  185.2 3.9 %collective-permute-start.14 = (f32[2,512,128]{2,1,0:T(8,128)}, f32[2,512,128]{2,1,0:T(8,128)}, u32[]{:S(2)}, u32[]{:S(2)}) collective-permute-start(f32[2,512,128]{2,1,0:T(8,128)} %bitcast.162), channel_id=1, source_target_pairs={{0,1},{1,2},{2,3},{3,4},{4,5},{5,6},{6,7},{7,8},{8,9},{9,10},{10,1... | collective-permute-start | bytes 1572872 | tf_op jit(solution)/shard_map/ppermute | solution.py:175
  191.4 4.5 %collective-permute-start.15 = (f32[2,512,128]{2,1,0:T(8,128)}, f32[2,512,128]{2,1,0:T(8,128)}, u32[]{:S(2)}, u32[]{:S(2)}) collective-permute-start(f32[2,512,128]{2,1,0:T(8,128)} %bitcast.161), channel_id=1, source_target_pairs={{0,2},{1,3},{2,4},{3,5},{4,6},{5,7},{6,8},{7,9},{8,10},{9,11},{10,... | collective-permute-start | bytes 1572872 | tf_op jit(solution)/shard_map/ppermute | solution.py:175
  199.3 3.0 %gather_fusion.1 = bf16[8,512,128]{2,1,0:T(8,128)(2,1)} fusion(bf16[10,512,128]{2,1,0:T(8,128)(2,1)} %constant_dynamic-update-slice_fusion.5, s32[1024]{0:T(1024)S(1)} %pad_clamp_fusion), kind=kCustom, calls=%fused_computation.1.clone | custom fusion | bytes 2097184 | tf_op jit(solution)/shard_map/jit(_take)/gather | solution.py:239
  203.7 4.2 %convolution_bitcast_fusion.4 = f32[2,512,128]{2,1,0:T(8,128)} fusion(bf16[2,512,2048]{2,1,0:T(8,128)(2,1)} %param.13, bf16[2,2048,128]{2,1,0:T(8,128)(2,1)S(1)} %bitcast.174), kind=kOutput, calls=%fused_computation.36 | convolution fusion | flops 536870912 | bytes 5767168 | tf_op jit(solution)/shard_map/cpk,ckm->cpm/dot_general | solution.py:240
  207.9 2.7 %convolution_convert_fusion = bf16[128,4096]{1,0:T(8,128)(2,1)} fusion(bf16[16,8,4096]{2,1,0:T(8,128)(2,1)} %all-to-all-done.1, s32[128]{0:T(128)S(1)} %multiply_add_fusion), kind=kOutput, calls=%fused_computation.2 | convolution fusion | flops 134758400 | bytes 2097664 | tf_op jit(solution)/shard_map/dot_general | solution.py:265
  210.6 2.3 reshape.132
  212.9 3.8 %convolution_bitcast_fusion.3 = f32[2,512,128]{2,1,0:T(8,128)S(1)} fusion(bf16[2,512,2048]{2,1,0:T(8,128)(2,1)} %param.16, bf16[2,2048,128]{2,1,0:T(8,128)(2,1)} %reshape.132), kind=kOutput, calls=%fused_computation.35 | convolution fusion | flops 536870912 | bytes 5767168 | tf_op jit(solution)/shard_map/cpk,ckm->cpm/dot_general | solution.py:269
  217.6 2.2 fusion.13
  220.4 33.6 %shard_map.96 = f32[128,128]{1,0:T(8,128)S(1)} custom-call(f32[16,8,128]{2,1,0:T(8,128)S(1)} %fusion.24.part, f32[128,128]{1,0:T(8,128)S(1)} %get-tuple-element.8.current), custom_call_target="tpu_custom_call" | custom-call | tf_op jit(solution)/shard_map/pallas_call | solution.py:159
  (111 shorter events, 61.9 us)
Async XLA Ops:
  0.6 47.5 %copy-start = (bf16[2,512,512]{2,1,0:T(8,128)(2,1)S(1)}, bf16[2,512,512]{2,1,0:T(8,128)(2,1)}, u32[]{:S(2)}) copy-start(bf16[2,512,512]{2,1,0:T(8,128)(2,1)} %param.12) | copy-start | bytes 3145732
  1.8 48.6 %collective-permute-start = (bf16[2,512,128]{2,1,0:T(8,128)(2,1)S(1)}, bf16[2,512,128]{2,1,0:T(8,128)(2,1)}, u32[]{:S(2)}, u32[]{:S(2)}) collective-permute-start(bf16[2,512,128]{2,1,0:T(8,128)(2,1)S(1)} %convert_element_type.32), channel_id=1, source_target_pairs={{0,2},{1,3},{2,4},{3,5},{4,6},{5,7},{6,8},{7,9},{8,10},{9,11},{10,... | collective-permute-start | bytes 786440 | tf_op jit(solution)/shard_map/ppermute | solution.py:175
  7.4 46.0 %collective-permute-start.1 = (bf16[2,512,128]{2,1,0:T(8,128)(2,1)S(1)}, bf16[2,512,128]{2,1,0:T(8,128)(2,1)}, u32[]{:S(2)}, u32[]{:S(2)}) collective-permute-start(bf16[2,512,128]{2,1,0:T(8,128)(2,1)S(1)} %convert_element_type.32), channel_id=1, source_target_pairs={{0,1},{1,2},{2,3},{3,4},{4,5},{5,6},{6,7},{7,8},{8,9},{9,10},{10,1... | collective-permute-start | bytes 786440 | tf_op jit(solution)/shard_map/ppermute | solution.py:175
  9.5 50.1 %collective-permute-start.2 = (bf16[2,512,128]{2,1,0:T(8,128)(2,1)S(1)}, bf16[2,512,128]{2,1,0:T(8,128)(2,1)}, u32[]{:S(2)}, u32[]{:S(2)}) collective-permute-start(bf16[2,512,128]{2,1,0:T(8,128)(2,1)S(1)} %convert_element_type.32), channel_id=1, source_target_pairs={{1,0},{2,1},{3,2},{4,3},{5,4},{6,5},{7,6},{8,7},{9,8},{10,9},{11,1... | collective-permute-start | bytes 786440 | tf_op jit(solution)/shard_map/ppermute | solution.py:175
  10.8 55.0 %collective-permute-start.3 = (bf16[2,512,128]{2,1,0:T(8,128)(2,1)S(1)}, bf16[2,512,128]{2,1,0:T(8,128)(2,1)}, u32[]{:S(2)}, u32[]{:S(2)}) collective-permute-start(bf16[2,512,128]{2,1,0:T(8,128)(2,1)S(1)} %convert_element_type.32), channel_id=1, source_target_pairs={{2,0},{3,1},{4,2},{5,3},{6,4},{7,5},{8,6},{9,7},{10,8},{11,9},{12,... | collective-permute-start | bytes 786440 | tf_op jit(solution)/shard_map/ppermute | solution.py:175
  20.5 53.6 %all-to-all-start = ((bf16[16,8,4096]{2,1,0:T(8,128)(2,1)}), bf16[16,8,4096]{2,1,0:T(8,128)(2,1)}, u32[]{:S(2)}, u32[]{:S(2)}) async-start(bf16[16,8,4096]{2,1,0:T(8,128)(2,1)} %fusion), calls=%async_computation | async-start | bytes 2097152 | tf_op jit(solution)/shard_map/all_to_all | solution.py:262
  35.9 3.3 %copy-start.15 = (s32[8]{0:T(128)S(1)}, s32[8]{0:T(128)}, u32[]{:S(2)}) copy-start(s32[8]{0:T(128)} %param.15) | copy-start | bytes 100
  35.9 3.3 %copy-start.16 = (s32[8]{0:T(128)S(1)}, s32[8]{0:T(128)}, u32[]{:S(2)}) copy-start(s32[8]{0:T(128)} %param.14) | copy-start | bytes 100
  39.2 6.4 %copy-start.12 = (s32[8]{0:T(128)}, s32[8]{0:T(128)S(1)}, u32[]{:S(2)}) copy-start(s32[8]{0:T(128)S(1)} %get-tuple-element.12) | copy-start | bytes 100
  44.4 36.6 %collective-permute-start.4 = (f32[2,512,128]{2,1,0:T(8,128)}, f32[2,512,128]{2,1,0:T(8,128)}, u32[]{:S(2)}, u32[]{:S(2)}) collective-permute-start(f32[2,512,128]{2,1,0:T(8,128)} %bitcast.168), channel_id=1, source_target_pairs={{2,0},{3,1},{4,2},{5,3},{6,4},{7,5},{8,6},{9,7},{10,8},{11,9},{12,... | collective-permute-start | bytes 1572872 | tf_op jit(solution)/shard_map/ppermute | solution.py:175
  46.5 2.9 %copy-start.2 = (f32[2,512,128]{2,1,0:T(8,128)S(1)}, f32[2,512,128]{2,1,0:T(8,128)}, u32[]{:S(2)}) copy-start(f32[2,512,128]{2,1,0:T(8,128)} %param.10) | copy-start | bytes 1572868
  50.4 30.5 %collective-permute-start.5 = (f32[2,512,128]{2,1,0:T(8,128)}, f32[2,512,128]{2,1,0:T(8,128)}, u32[]{:S(2)}, u32[]{:S(2)}) collective-permute-start(f32[2,512,128]{2,1,0:T(8,128)} %bitcast.167), channel_id=1, source_target_pairs={{1,0},{2,1},{3,2},{4,3},{5,4},{6,5},{7,6},{8,7},{9,8},{10,9},{11,1... | collective-permute-start | bytes 1572872 | tf_op jit(solution)/shard_map/ppermute | solution.py:175
  53.4 27.5 %collective-permute-start.6 = (f32[2,512,128]{2,1,0:T(8,128)}, f32[2,512,128]{2,1,0:T(8,128)}, u32[]{:S(2)}, u32[]{:S(2)}) collective-permute-start(f32[2,512,128]{2,1,0:T(8,128)} %bitcast.166), channel_id=1, source_target_pairs={{0,1},{1,2},{2,3},{3,4},{4,5},{5,6},{6,7},{7,8},{8,9},{9,10},{10,1... | collective-permute-start | bytes 1572872 | tf_op jit(solution)/shard_map/ppermute | solution.py:175
  59.6 21.3 %collective-permute-start.7 = (f32[2,512,128]{2,1,0:T(8,128)}, f32[2,512,128]{2,1,0:T(8,128)}, u32[]{:S(2)}, u32[]{:S(2)}) collective-permute-start(f32[2,512,128]{2,1,0:T(8,128)} %bitcast.165), channel_id=1, source_target_pairs={{0,2},{1,3},{2,4},{3,5},{4,6},{5,7},{6,8},{7,9},{8,10},{9,11},{10,... | collective-permute-start | bytes 1572872 | tf_op jit(solution)/shard_map/ppermute | solution.py:175
  77.1 3.9 %copy-start.6 = (f32[2,512,128]{2,1,0:T(8,128)S(1)}, f32[2,512,128]{2,1,0:T(8,128)}, u32[]{:S(2)}) copy-start(f32[2,512,128]{2,1,0:T(8,128)} %fusion.39) | copy-start | bytes 1572868
  77.1 3.9 %copy-start.9 = (f32[2,512,128]{2,1,0:T(8,128)S(1)}, f32[2,512,128]{2,1,0:T(8,128)}, u32[]{:S(2)}) copy-start(f32[2,512,128]{2,1,0:T(8,128)} %convolution_bitcast_fusion.6) | copy-start | bytes 1572868
  77.1 3.9 %copy-start.11 = (f32[2,512]{1,0:T(2,128)S(1)}, f32[2,512]{1,0:T(2,128)}, u32[]{:S(2)}) copy-start(f32[2,512]{1,0:T(2,128)} %param.11) | copy-start | bytes 12292
  124.5 14.1 %copy-start.1 = (bf16[2,512,2048]{2,1,0:T(8,128)(2,1)S(1)}, bf16[2,512,2048]{2,1,0:T(8,128)(2,1)}, u32[]{:S(2)}) copy-start(bf16[2,512,2048]{2,1,0:T(8,128)(2,1)} %param.16) | copy-start | bytes 12582916
  124.5 57.7 %collective-permute-start.8 = (bf16[2,512,128]{2,1,0:T(8,128)(2,1)S(1)}, bf16[2,512,128]{2,1,0:T(8,128)(2,1)}, u32[]{:S(2)}, u32[]{:S(2)}) collective-permute-start(bf16[2,512,128]{2,1,0:T(8,128)(2,1)S(1)} %get-tuple-element.9), channel_id=1, source_target_pairs={{0,2},{1,3},{2,4},{3,5},{4,6},{5,7},{6,8},{7,9},{8,10},{9,11},{10,... | collective-permute-start | bytes 786440 | tf_op jit(solution)/shard_map/ppermute | solution.py:175
  129.0 56.2 %collective-permute-start.9 = (bf16[2,512,128]{2,1,0:T(8,128)(2,1)S(1)}, bf16[2,512,128]{2,1,0:T(8,128)(2,1)}, u32[]{:S(2)}, u32[]{:S(2)}) collective-permute-start(bf16[2,512,128]{2,1,0:T(8,128)(2,1)S(1)} %get-tuple-element.9), channel_id=1, source_target_pairs={{0,1},{1,2},{2,3},{3,4},{4,5},{5,6},{6,7},{7,8},{8,9},{9,10},{10,1... | collective-permute-start | bytes 786440 | tf_op jit(solution)/shard_map/ppermute | solution.py:175
  131.5 59.9 %collective-permute-start.10 = (bf16[2,512,128]{2,1,0:T(8,128)(2,1)S(1)}, bf16[2,512,128]{2,1,0:T(8,128)(2,1)}, u32[]{:S(2)}, u32[]{:S(2)}) collective-permute-start(bf16[2,512,128]{2,1,0:T(8,128)(2,1)S(1)} %get-tuple-element.9), channel_id=1, source_target_pairs={{1,0},{2,1},{3,2},{4,3},{5,4},{6,5},{7,6},{8,7},{9,8},{10,9},{11,1... | collective-permute-start | bytes 786440 | tf_op jit(solution)/shard_map/ppermute | solution.py:175
  132.8 64.8 %collective-permute-start.11 = (bf16[2,512,128]{2,1,0:T(8,128)(2,1)S(1)}, bf16[2,512,128]{2,1,0:T(8,128)(2,1)}, u32[]{:S(2)}, u32[]{:S(2)}) collective-permute-start(bf16[2,512,128]{2,1,0:T(8,128)(2,1)S(1)} %get-tuple-element.9), channel_id=1, source_target_pairs={{2,0},{3,1},{4,2},{5,3},{6,4},{7,5},{8,6},{9,7},{10,8},{11,9},{12,... | collective-permute-start | bytes 786440 | tf_op jit(solution)/shard_map/ppermute | solution.py:175
  143.3 3.4 %copy-start.13 = (s32[8]{0:T(128)S(1)}, s32[8]{0:T(128)}, u32[]{:S(2)}) copy-start(s32[8]{0:T(128)} %copy-done.12) | copy-start | bytes 100
  159.2 48.7 %all-to-all-start.1 = ((bf16[16,8,4096]{2,1,0:T(8,128)(2,1)}), bf16[16,8,4096]{2,1,0:T(8,128)(2,1)}, u32[]{:S(2)}, u32[]{:S(2)}) async-start(bf16[16,8,4096]{2,1,0:T(8,128)(2,1)} %fusion.1), calls=%async_computation.1 | async-start | bytes 2097152 | tf_op jit(solution)/shard_map/all_to_all | solution.py:262
  175.2 41.6 %collective-permute-start.12 = (f32[2,512,128]{2,1,0:T(8,128)}, f32[2,512,128]{2,1,0:T(8,128)}, u32[]{:S(2)}, u32[]{:S(2)}) collective-permute-start(f32[2,512,128]{2,1,0:T(8,128)} %bitcast.164), channel_id=1, source_target_pairs={{2,0},{3,1},{4,2},{5,3},{6,4},{7,5},{8,6},{9,7},{10,8},{11,9},{12,... | collective-permute-start | bytes 1572872 | tf_op jit(solution)/shard_map/ppermute | solution.py:175
  182.2 34.6 %collective-permute-start.13 = (f32[2,512,128]{2,1,0:T(8,128)}, f32[2,512,128]{2,1,0:T(8,128)S(1)}, u32[]{:S(2)}, u32[]{:S(2)}) collective-permute-start(f32[2,512,128]{2,1,0:T(8,128)} %bitcast.163), channel_id=1, source_target_pairs={{1,0},{2,1},{3,2},{4,3},{5,4},{6,5},{7,6},{8,7},{9,8},{10,9},{11,1... | collective-permute-start | bytes 1572872 | tf_op jit(solution)/shard_map/ppermute | solution.py:175
  185.2 31.6 %collective-permute-start.14 = (f32[2,512,128]{2,1,0:T(8,128)}, f32[2,512,128]{2,1,0:T(8,128)}, u32[]{:S(2)}, u32[]{:S(2)}) collective-permute-start(f32[2,512,128]{2,1,0:T(8,128)} %bitcast.162), channel_id=1, source_target_pairs={{0,1},{1,2},{2,3},{3,4},{4,5},{5,6},{6,7},{7,8},{8,9},{9,10},{10,1... | collective-permute-start | bytes 1572872 | tf_op jit(solution)/shard_map/ppermute | solution.py:175
  191.4 25.4 %collective-permute-start.15 = (f32[2,512,128]{2,1,0:T(8,128)}, f32[2,512,128]{2,1,0:T(8,128)}, u32[]{:S(2)}, u32[]{:S(2)}) collective-permute-start(f32[2,512,128]{2,1,0:T(8,128)} %bitcast.161), channel_id=1, source_target_pairs={{0,2},{1,3},{2,4},{3,5},{4,6},{5,7},{6,8},{7,9},{8,10},{9,11},{10,... | collective-permute-start | bytes 1572872 | tf_op jit(solution)/shard_map/ppermute | solution.py:175
  212.9 4.7 %copy-start.5 = (f32[1,2,512,128]{3,1,2,0:T(2,128)S(1)}, f32[1,2,512,128]{3,1,2,0:T(2,128)}, u32[]{:S(2)}) copy-start(f32[1,2,512,128]{3,1,2,0:T(2,128)} %get-tuple-element.13) | copy-start | bytes 1572868
  212.9 4.7 %copy-start.7 = (f32[2,128,512]{1,2,0:T(8,128)S(1)}, f32[2,128,512]{1,2,0:T(8,128)}, u32[]{:S(2)}) copy-start(f32[2,128,512]{1,2,0:T(8,128)} %fusion.41) | copy-start | bytes 1572868
  212.9 4.7 %copy-start.8 = (f32[2,512,128]{2,1,0:T(8,128)S(1)}, f32[2,512,128]{2,1,0:T(8,128)}, u32[]{:S(2)}) copy-start(f32[2,512,128]{2,1,0:T(8,128)} %convolution_bitcast_fusion.4) | copy-start | bytes 1572868
  217.6 36.5 %copy-start.3 = (f32[2,512,128]{2,1,0:T(8,128)S(1)}, f32[2,512,128]{2,1,0:T(8,128)}, u32[]{:S(2)}) copy-start(f32[2,512,128]{2,1,0:T(8,128)} %get-tuple-element.23) | copy-start | bytes 1572868
  (3 other events, 4.5 us)
where the time goes:
time: 258 us; the launch traced here: 257 us
  Pallas kernels  70.6 us (27%)
  matrix products  65.7 us (25%)
  starting transfers between devices  61.4 us (24%)
  local copies, waits for them, and re-layouts  54.1 us (21%)
  other arithmetic  3.91 us (2%)
    pallas_call x2, Pallas kernels, solve_call(): pl.pallas_call(functools.partial(kernel, devices), out_shape=[square] * o...  70.6 us
    ppermute x16, starting transfers between devices, from_behind(): lax.ppermute(value, axis, [(source, source + steps) for source in range(l...  42 us
    unnamed x51, local copies, waits for them, and re-layouts  25 us
    all_to_all x2, starting transfers between devices, shards(): lax.all_to_all(outgoing, 'clusters', split_axis=0, concat_axis=0, tiled=T...  19.4 us
    dot_general x2, matrix products, shards(): jnp.einsum('cpk,cpm->ckm', near_blocks, packed, preferred_element_type=jn...  9.55 us
    dot_general x2, matrix products, shards(): jnp.dot(window_table, mirrored, precision=lax.Precision.HIGHEST)  8.74 us
    dot_general x2, matrix products, shards(): jnp.einsum('cpk,ckm->cpm', near_blocks, fetched, preferred_element_type=j...  8.5 us
    dot_general x2, matrix products, shards(): jnp.einsum('cpk,ckm->cpm', far_factors, matched, preferred_element_type=j...  7.65 us
  transfers between devices with their start and end apart: 18, of which 0 were waited for; matrix products, arithmetic and copies ran while one was open for 43% of the time, Pallas kernels for 0%

commit v1 on v0

v1 whole, which is shorter than its diff:
```python
import functools

import jax
import jax.numpy as jnp
from jax import lax
from jax.experimental import pallas as pl
from jax.experimental.pallas import tpu as pltpu
from jax.sharding import PartitionSpec as P

MESH = pl.DeviceIdType.MESH
RANK = 32
REACH = 2
ITERS = 2
HIGH = lax.Precision.HIGHEST


def hdot(left, right, dims=((1,), (0,))):
    return lax.dot_general(left, right, (dims, ((), ())), precision=HIGH, preferred_element_type=jnp.float32)


def invert(mats):
    size = mats[0].shape[0]
    rows = lax.broadcasted_iota(jnp.int32, (size, size), 0)
    lanes = lax.broadcasted_iota(jnp.int32, (size, size), 1)

    def body(_, mats):
        done = []
        for a in mats:
            for k in range(8):
                column = a[:, k : k + 1]
                pivot = 1.0 / a[k : k + 1, k : k + 1]
                line = jnp.where(lanes[:1] == k, pivot, a[k : k + 1] * pivot)
                a = jnp.where(rows == k, line, jnp.where(lanes == k, 0.0, a) - column * line)
            a = pltpu.roll(a, size - 8, 1)
            done.append(jnp.concatenate([a[8:], a[:8]], axis=0))
        return tuple(done)

    return lax.fori_loop(0, size // 8, body, tuple(mats))


def meet(devices):
    me = lax.axis_index("clusters")
    barrier = pltpu.get_barrier_semaphore()

    def greet(k, carry):
        peer = lax.rem(me + k, devices)
        pl.semaphore_signal(barrier, inc=1, device_id={"clusters": peer}, device_id_type=MESH)
        return carry

    lax.fori_loop(1, devices, greet, 0)
    pl.semaphore_wait(barrier, devices - 1)


def reduce_all(devices, part, landing, total, sems):
    me = lax.axis_index("clusters")
    pieces = part.shape[0]
    send_a, recv_a, send_b, recv_b = sems

    def copy_a(k, peer):
        return pltpu.make_async_remote_copy(
            src_ref=part.at[peer], dst_ref=landing.at[k], send_sem=send_a.at[k], recv_sem=recv_a.at[k],
            device_id={"clusters": peer}, device_id_type=MESH)

    def copy_b(k, peer, piece):
        return pltpu.make_async_remote_copy(
            src_ref=total.at[piece], dst_ref=total.at[piece], send_sem=send_b.at[k], recv_sem=recv_b.at[k],
            device_id={"clusters": peer}, device_id_type=MESH)

    def loop(fn):
        def body(k, carry):
            fn(k)
            return carry
        lax.fori_loop(1, devices, body, 0)

    def send_one(k):
        peer = lax.rem(me + k, devices)
        if pieces == devices:
            copy_a(k, peer).start()
        else:
            @pl.when(peer < pieces)
            def _():
                copy_a(k, peer).start()

    loop(send_one)

    def gather():
        def add(k, acc):
            copy_a(k, 0).wait_recv()
            return acc + landing[k]
        total[me] = lax.fori_loop(1, devices, add, part[me])
        loop(lambda k: copy_b(k, lax.rem(me + k, devices), me).start())

    if pieces == devices:
        gather()
    else:
        pl.when(me < pieces)(gather)

    def arrive(k):
        origin = lax.rem(me - k + devices, devices)
        if pieces == devices:
            copy_b(k, 0, origin).wait_recv()
        else:
            @pl.when(origin < pieces)
            def _():
                copy_b(k, 0, origin).wait_recv()

    loop(arrive)

    def finish(k):
        peer = lax.rem(me + k, devices)
        if pieces == devices:
            copy_a(k, peer).wait_send()
            copy_b(k, peer, me).wait_send()
        else:
            @pl.when(peer < pieces)
            def _():
                copy_a(k, peer).wait_send()

            @pl.when(me < pieces)
            def _():
                copy_b(k, peer, me).wait_send()

    loop(finish)


def symmetric(mat):
    return 0.5 * (mat + mat.T)


def fast_dot(left, right):
    return jnp.dot(left, right, preferred_element_type=jnp.float32)


def times(count, fn):
    def body(k, carry):
        fn(k)
        return carry
    lax.fori_loop(0, count, body, 0)


def kernel(
    devices, right_ref, diag_ref, self_hbm, near_hbm, far_hbm, offset_ref, column_ref, peer_ref, rank_ref, source_ref,
    field_ref, resid_ref,
    own, near, far, direction, image, turned, window, window_sems, mirrored, returned, landed, mirror_sems,
    compressed, outgoing, incoming, far_send, far_recv, matched, part_a, landing_a, total_a, part_b, landing_b, total_b,
    load_sems, send_a, recv_a, send_b, recv_b,
):
    me = lax.axis_index("clusters")
    cl_dev, panels, modes = right_ref.shape
    near_cl = near.shape[2] // panels
    far_cl = far.shape[2] // RANK
    capacity = outgoing.shape[1]
    far_dev = cl_dev * far_cl
    offsets = [o for o in range(-REACH, REACH + 1) if o]
    sems = (send_a, recv_a, send_b, recv_b)

    loads = [
        pltpu.make_async_copy(far_hbm, far, load_sems.at[0]),
        pltpu.make_async_copy(near_hbm, near, load_sems.at[1]),
        pltpu.make_async_copy(self_hbm, own, load_sems.at[2]),
    ]
    for load in loads:
        load.start()

    def inside(offset):
        return (me + offset >= 0) & (me + offset < devices)

    for offset in offsets:
        @pl.when(jnp.logical_not(inside(offset)))
        def _():
            window[offset + REACH] = jnp.zeros(window.shape[1:], window.dtype)
    compressed[far_dev] = jnp.zeros(compressed.shape[1:], compressed.dtype)
    direction[...] = right_ref[...]
    resid_ref[...] = right_ref[...]
    meet(devices)

    def window_copy(offset):
        return pltpu.make_async_remote_copy(
            src_ref=window.at[REACH], dst_ref=window.at[REACH - offset],
            send_sem=window_sems.at[0, REACH + offset], recv_sem=window_sems.at[1, REACH - offset],
            device_id={"clusters": me + offset}, device_id_type=MESH)

    def window_from(offset):
        return pltpu.make_async_remote_copy(
            src_ref=window.at[REACH], dst_ref=window.at[REACH + offset],
            send_sem=window_sems.at[0, REACH + offset], recv_sem=window_sems.at[1, REACH + offset],
            device_id={"clusters": me + offset}, device_id_type=MESH)

    def mirror_copy(offset):
        return pltpu.make_async_remote_copy(
            src_ref=returned.at[REACH + offset], dst_ref=landed.at[REACH - offset],
            send_sem=mirror_sems.at[0, REACH + offset], recv_sem=mirror_sems.at[1, REACH - offset],
            device_id={"clusters": me + offset}, device_id_type=MESH)

    def mirror_from(offset):
        return pltpu.make_async_remote_copy(
            src_ref=returned.at[REACH + offset], dst_ref=landed.at[REACH + offset],
            send_sem=mirror_sems.at[0, REACH + offset], recv_sem=mirror_sems.at[1, REACH + offset],
            device_id={"clusters": me + offset}, device_id_type=MESH)

    def far_copy(k, peer, slot):
        return pltpu.make_async_remote_copy(
            src_ref=outgoing.at[peer], dst_ref=incoming.at[slot], send_sem=far_send.at[k], recv_sem=far_recv.at[k],
            device_id={"clusters": peer}, device_id_type=MESH)

    def when_inside(fn):
        for offset in offsets:
            @pl.when(inside(offset))
            def _():
                fn(offset)

    def operate(first):
        for c in range(cl_dev):
            value = direction[c]
            window[REACH, c] = value.astype(jnp.bfloat16)
            turned[c] = value.T.astype(jnp.bfloat16)
        when_inside(lambda o: window_copy(o).start())

        if first:
            loads[0].wait()
        tiles = far_cl * RANK // panels
        tile_halves = panels // RANK

        def compress(i):
            c, q = i // tiles, i % tiles
            columns = pl.ds(pl.multiple_of(q * panels, panels), panels)
            value = fast_dot(turned[c], far[c, :, columns]).T.astype(jnp.bfloat16)
            compressed[pl.ds(i * tile_halves, tile_halves)] = value.reshape(tile_halves, RANK, modes)

        times(cl_dev * tiles, compress)

        def post(k):
            peer = lax.rem(me + k, devices)
            for r in range(capacity):
                outgoing[peer, r] = compressed[source_ref[peer * capacity + r]]

        def send(k):
            post(k + 1)
            far_copy(k + 1, lax.rem(me + k + 1, devices), me).start()

        times(devices - 1, send)
        for r in range(capacity):
            incoming[me, r] = compressed[source_ref[me * capacity + r]]

        if first:
            loads[1].wait()

        def mirror(i):
            c, q = i // near_cl, i % near_cl
            columns = pl.ds(pl.multiple_of(q * panels, panels), panels)
            mirrored[i] = fast_dot(turned[c], near[c, :, columns]).T

        times(cl_dev * near_cl, mirror)

        for o in [1, -1, 2, -2, 0]:
            for c in range(cl_dev):
                hits = [
                    jnp.where((offset_ref[i] == o) & (column_ref[i] == c), 1.0, 0.0).astype(jnp.float32)
                    for i in range(cl_dev * near_cl)
                ]
                target = image.at[c] if o == 0 else returned.at[o + REACH, c]

                def fold(t):
                    rows = pl.ds(pl.multiple_of(t * 64, 64), 64)
                    total = mirrored[0, rows] * hits[0]
                    for i in range(1, cl_dev * near_cl):
                        total = total + mirrored[i, rows] * hits[i]
                    target[rows] = total

                times(panels // 64, fold)
            if o:
                @pl.when(inside(o))
                def _():
                    mirror_copy(o).start()

        if first:
            loads[2].wait()
        for c in range(cl_dev):
            both = fast_dot(own[c], window[REACH, c]) + fast_dot(turned[c], own[c]).T
            image[c] += 0.5 * both + diag_ref[c] * direction[c]

        when_inside(lambda o: window_from(o).wait_recv())

        def forward(i):
            c, q = i // near_cl, i % near_cl
            columns = pl.ds(pl.multiple_of(q * panels, panels), panels)
            image[c] += fast_dot(near[c, :, columns], window[offset_ref[i] + REACH, column_ref[i]])

        times(cl_dev * near_cl, forward)

        times(devices - 1, lambda k: far_copy(k + 1, me, lax.rem(me - k - 1 + devices, devices)).wait_recv())

        def match(i):
            for j in range(8):
                h = i * 8 + j
                matched[h] = incoming[peer_ref[h], rank_ref[h]]

        times(far_dev // 8, match)

        def expand(i):
            c, q = i // tiles, i % tiles
            columns = pl.ds(pl.multiple_of(q * panels, panels), panels)
            value = matched[pl.ds(i * tile_halves, tile_halves)].reshape(panels, modes)
            image[c] += fast_dot(far[c, :, columns], value)

        times(cl_dev * tiles, expand)

        def collect(o):
            mirror_from(o).wait_recv()
            image[...] += landed[REACH + o]

        when_inside(collect)

    def settle():
        when_inside(lambda o: window_copy(o).wait_send())
        when_inside(lambda o: mirror_copy(o).wait_send())
        times(devices - 1, lambda k: far_copy(k + 1, lax.rem(me + k + 1, devices), me).wait_send())

    def flat(ref):
        return ref[...].reshape(cl_dev * panels, modes)

    def combine(ref, coeff):
        return hdot(flat(ref), coeff).reshape(cl_dev, panels, modes)

    def gram(left, right):
        return hdot(flat(left).T, flat(right))

    operate(True)
    grams = jnp.concatenate([gram(direction, direction), gram(direction, image), gram(image, image)], axis=0)
    part_a[...] = grams.reshape(part_a.shape)
    reduce_all(devices, part_a, landing_a, total_a, sems)
    whole = total_a[...].reshape(-1, modes)
    current, curvature, squared = whole[:modes], whole[modes : 2 * modes], whole[2 * modes :]
    inv_curv, inv_cur = invert([symmetric(curvature), symmetric(current)])
    step = hdot(inv_curv, current)
    cross = hdot(curvature, step)
    later = current - cross - cross.T + hdot(step.T, hdot(squared, step))
    blend = hdot(inv_cur, later)
    field_ref[...] = combine(direction, step)
    resid_ref[...] = resid_ref[...] - combine(image, step)
    direction[...] = resid_ref[...] + combine(direction, blend)
    settle()

    operate(False)
    part_b[...] = gram(direction, image).reshape(part_b.shape)
    reduce_all(devices, part_b, landing_b, total_b, sems)
    (inv_curv,) = invert([symmetric(total_b[...].reshape(modes, modes))])
    step = hdot(inv_curv, later)
    field_ref[...] = field_ref[...] + combine(direction, step)
    resid_ref[...] = resid_ref[...] - combine(image, step)
    settle()


def shards(
    right_side, diag_shift, self_blocks, near_blocks, near_offset, near_column, far_factors, far_peer
):
    cl_dev, panels, modes = right_side.shape
    devices = lax.axis_size("clusters")
    far_dev = far_peer.shape[0]
    near_cl = near_blocks.shape[2] // panels
    capacity = max(2, -(-far_dev // devices))
    peers = far_peer[:, 0]
    hot = (peers[:, None] == jnp.arange(devices, dtype=jnp.int32)[None, :]).astype(jnp.int32)
    rank = jnp.sum((jnp.cumsum(hot, axis=0) - hot) * hot, axis=1)
    slot = (peers * capacity + rank)[None, :] == jnp.arange(devices * capacity, dtype=jnp.int32)[:, None]
    halves = jnp.arange(far_dev, dtype=jnp.int32)[None, :]
    source = far_dev + jnp.sum(jnp.where(slot, halves - far_dev, 0), axis=1)
    diag = jnp.broadcast_to(diag_shift[:, :, None], right_side.shape)
    span = 2 * REACH + 1
    block = (cl_dev, panels, modes)
    shape_a = (min(devices, 3 * modes // 8), 3 * modes // min(devices, 3 * modes // 8), modes)
    shape_b = (min(devices, modes // 8), modes // min(devices, modes // 8), modes)
    half = (RANK, modes)
    f32, bf16, dma = jnp.float32, jnp.bfloat16, pltpu.SemaphoreType.DMA
    vmem = pl.BlockSpec(memory_space=pltpu.VMEM)
    smem = pl.BlockSpec(memory_space=pltpu.SMEM)
    anywhere = pl.BlockSpec(memory_space=pl.ANY)
    macs = 2 * 2 * cl_dev * panels * modes * 2 * (panels + near_blocks.shape[2] + far_factors.shape[2])
    return pl.pallas_call(
        functools.partial(kernel, devices),
        out_shape=[jax.ShapeDtypeStruct(block, f32)] * 2,
        in_specs=[vmem] * 2 + [anywhere] * 3 + [smem] * 5,
        out_specs=[vmem] * 2,
        scratch_shapes=[
            pltpu.VMEM(self_blocks.shape, bf16),
            pltpu.VMEM(near_blocks.shape, bf16),
            pltpu.VMEM(far_factors.shape, bf16),
            pltpu.VMEM(block, f32),
            pltpu.VMEM(block, f32),
            pltpu.VMEM((cl_dev, modes, panels), bf16),
            pltpu.VMEM((span,) + block, bf16),
            dma((2, span)),
            pltpu.VMEM((cl_dev * near_cl, panels, modes), f32),
            pltpu.VMEM((span,) + block, f32),
            pltpu.VMEM((span,) + block, f32),
            dma((2, span)),
            pltpu.VMEM((far_dev + 1,) + half, bf16),
            pltpu.VMEM((devices, capacity) + half, bf16),
            pltpu.VMEM((devices, capacity) + half, bf16),
            dma((devices,)),
            dma((devices,)),
            pltpu.VMEM((far_dev,) + half, bf16),
            pltpu.VMEM(shape_a, f32),
            pltpu.VMEM((devices,) + shape_a[1:], f32),
            pltpu.VMEM(shape_a, f32),
            pltpu.VMEM(shape_b, f32),
            pltpu.VMEM((devices,) + shape_b[1:], f32),
            pltpu.VMEM(shape_b, f32),
            dma((3,)),
        ] + [dma((devices,))] * 4,
        compiler_params=pltpu.CompilerParams(collective_id=1, has_side_effects=True, vmem_limit_bytes=48 << 20),
        cost_estimate=pl.CostEstimate(flops=2 * macs, bytes_accessed=12 << 20, transcendentals=0),
    )(right_side, diag, self_blocks, near_blocks, far_factors, near_offset, near_column, peers, rank, source)


def solution(mesh):
    in_specs = (
        P(("groups", "clusters"), None, None),
        P(("groups", "clusters"), None),
        P(("groups", "clusters"), None, None),
        P(("groups", "clusters"), None, None),
        P(("groups", "clusters")),
        P(("groups", "clusters")),
        P(("groups", "clusters"), None, None),
        P(("groups", "clusters"), None),
    )
    out_specs = (P(("groups", "clusters"), None, None), P(("groups", "clusters"), None, None))
    return jax.shard_map(shards, mesh=mesh, in_specs=in_specs, out_specs=out_specs, check_vma=False)
```

time: 258 us -> 197 us (0.76)
  Pallas kernels: 70.6 us -> 186 us
  matrix products: 65.7 us -> 0 us
  starting transfers between devices: 61.4 us -> 0 us
  local copies, waits for them, and re-layouts: 54.1 us -> 6.7 us
    pallas_call x2 -> x1, Pallas kernels: 70.6 us -> 186 us  [shards(): pl.pallas_call(functools.partial(kernel, devices), out_shape=[jax.ShapeDt...]
    dot_general x27 -> x0, matrix products: 65.7 us -> none  [the longest x2 9.55 us: shards(): jnp.einsum('cpk,cpm->ckm', near_blocks, packed, preferred_element_type=jn...]
    ppermute x16 -> x0, starting transfers between devices: 42 us -> none  [from_behind(): lax.ppermute(value, axis, [(source, source + steps) for source in range(l...]
    all_to_all x2 -> x0, starting transfers between devices: 19.4 us -> none  [shards(): lax.all_to_all(outgoing, 'clusters', split_axis=0, concat_axis=0, tiled=T...]
    unnamed x51 -> x12, local copies, waits for them, and re-layouts: 25 us -> 5.82 us
    reshape x7 -> x0, local copies, waits for them, and re-layouts: 14.3 us -> none  [the longest x2 6.69 us: shards(): mirrored = mirrored.reshape(cl_dev * near_cl, panels * modes)]
    gather x2 -> x0, local copies, waits for them, and re-layouts: 5.04 us -> none  [shards(): jnp.take(window, window_pos, axis=0)]
    dot_general x3 -> x0, local copies, waits for them, and re-layouts: 4.07 us -> none  [the longest x1 2.88 us: shards(): jnp.einsum('cpk,cpm->ckm', near_blocks, packed, preferred_element_type=jn...]
  transfers between devices with their start and end apart: 18 -> 0, of which waited for: 0 -> 0; matrix products, arithmetic and copies ran while one was open for 43% -> 0% of each run, Pallas kernels for 0% -> 0%
where the time goes in v1:
time: 197 us; the launch traced here: 196 us
  Pallas kernels  186 us (94%)
  local copies, waits for them, and re-layouts  6.7 us (3%)
  other arithmetic  2.51 us (1%)
    pallas_call x1, Pallas kernels, shards(): pl.pallas_call(functools.partial(kernel, devices), out_shape=[jax.ShapeDt...  186 us
    unnamed x12, local copies, waits for them, and re-layouts  5.82 us

profile of v1, /device:TPU:0, one launch (start us, length us, event | category | flops | bytes accessed | tf_op | source)
XLA Modules:
  0.0 196.3 jit_solution(1651798631083556555)
XLA Ops:
  0.6 0.7 fusion
  1.4 0.2 reduce_window_sum.11
  1.5 0.8 select_reduce_fusion.1.rank_ref
  2.4 0.7 iota_add_fusion
  3.0 0.1 select_reduce_fusion
  3.2 0.9 broadcast_in_dim.14.diag_ref
  4.1 0.0 copy-start
  4.1 0.6 copy-done
  4.7 0.0 copy-start.1
  4.7 1.2 copy-done.1
  5.9 0.0 copy-start.2
  5.9 1.0 copy-done.2
  7.0 0.0 copy-start.3
  7.0 0.7 copy-done.3
  7.6 0.0 copy-start.4
  7.6 0.7 copy-done.4
  8.3 186.4 %shard_map.95 = (f32[2,512,128]{2,1,0:T(8,128)S(1)}, f32[2,512,128]{2,1,0:T(8,128)S(1)}) custom-call(f32[2,512,128]{2,1,0:T(8,128)S(1)} %copy-done.2, f32[2,512,128]{2,1,0:T(8,128)S(1)} %broadcast_in_dim.14.diag_ref, bf16[2,512,512]{2,1,0:T(8,128)(2,1)S(1)} %copy-done.1, bf16[2,512,2048]{2,1,0:T(8,128)(2,1)} %near_hbm.1, bf16[2,512,2048]{2,1,0:T(8,128)(2,1)} %far_hbm.1, ...), custom_call_target="tpu_custom_call" | custom-call | flops 9663676416 | bytes 12582912 | tf_op jit(solution)/shard_map/pallas_call | solution.py:379
  194.7 0.8 copy.12
  195.5 0.8 copy.13
  (1 shorter events, 0.0 us)
Async XLA Ops:
  4.1 0.7 copy-start
  4.7 1.2 copy-start.1
  5.9 1.0 copy-start.2
  7.0 0.7 copy-start.3
  7.6 0.7 copy-start.4

commit v2 on v1

--- a/solution.py
+++ b/solution.py
@@ -10,7 +10,7 @@
 MESH = pl.DeviceIdType.MESH
 RANK = 32
 REACH = 2
-ITERS = 2
+STEPS = 32000.0
 HIGH = lax.Precision.HIGHEST
 
 
@@ -141,7 +141,7 @@
 def kernel(
     devices, right_ref, diag_ref, self_hbm, near_hbm, far_hbm, offset_ref, column_ref, peer_ref, rank_ref, source_ref,
     field_ref, resid_ref,
-    own, near, far, direction, image, turned, window, window_sems, mirrored, returned, landed, mirror_sems,
+    own, near, far, direction, image, turned, window, window_sems, mirrored, returned, landed, scale_out, scale_in, stage, partial, partner, mirror_sems,
     compressed, outgoing, incoming, far_send, far_recv, matched, part_a, landing_a, total_a, part_b, landing_b, total_b,
     load_sems, send_a, recv_a, send_b, recv_b,
 ):
@@ -153,6 +153,8 @@
     far_dev = cl_dev * far_cl
     offsets = [o for o in range(-REACH, REACH + 1) if o]
     sems = (send_a, recv_a, send_b, recv_b)
+    odd = lax.rem(me, 2)
+    beside, across, joint = 1 - 2 * odd, 4 * odd - 2, 2 * odd - 1
 
     loads = [
         pltpu.make_async_copy(far_hbm, far, load_sems.at[0]),
@@ -186,17 +188,36 @@
             send_sem=window_sems.at[0, REACH + offset], recv_sem=window_sems.at[1, REACH + offset],
             device_id={"clusters": me + offset}, device_id_type=MESH)
 
-    def mirror_copy(offset):
-        return pltpu.make_async_remote_copy(
-            src_ref=returned.at[REACH + offset], dst_ref=landed.at[REACH - offset],
-            send_sem=mirror_sems.at[0, REACH + offset], recv_sem=mirror_sems.at[1, REACH - offset],
-            device_id={"clusters": me + offset}, device_id_type=MESH)
-
-    def mirror_from(offset):
-        return pltpu.make_async_remote_copy(
-            src_ref=returned.at[REACH + offset], dst_ref=landed.at[REACH + offset],
-            send_sem=mirror_sems.at[0, REACH + offset], recv_sem=mirror_sems.at[1, REACH + offset],
-            device_id={"clusters": me + offset}, device_id_type=MESH)
+    def window_relay(side):
+        return pltpu.make_async_remote_copy(
+            src_ref=window.at[REACH + side], dst_ref=window.at[REACH + 2 * side],
+            send_sem=window_sems.at[0, REACH], recv_sem=window_sems.at[1, REACH + 2 * side],
+            device_id={"clusters": me - side}, device_id_type=MESH)
+
+    def partial_copy():
+        return pltpu.make_async_remote_copy(
+            src_ref=partial, dst_ref=partner, send_sem=mirror_sems.at[0, 3], recv_sem=mirror_sems.at[1, 3],
+            device_id={"clusters": me + beside}, device_id_type=MESH)
+
+    def mirror_copy(kind):
+        return pltpu.make_async_remote_copy(
+            src_ref=returned.at[kind], dst_ref=landed.at[kind],
+            send_sem=mirror_sems.at[0, kind], recv_sem=mirror_sems.at[1, kind],
+            device_id={"clusters": me + (beside, across, joint)[kind]}, device_id_type=MESH)
+
+    def scale_copy(kind):
+        return pltpu.make_async_remote_copy(
+            src_ref=scale_out.at[kind], dst_ref=scale_in.at[kind],
+            send_sem=mirror_sems.at[0, 4 + kind], recv_sem=mirror_sems.at[1, 4 + kind],
+            device_id={"clusters": me + (beside, across, joint)[kind]}, device_id_type=MESH)
+
+    def post_mirror(kind):
+        mirror_copy(kind).start()
+        scale_copy(kind).start()
+
+    def sent_mirror(kind):
+        mirror_copy(kind).wait_send()
+        scale_copy(kind).wait_send()
 
     def far_copy(k, peer, slot):
         return pltpu.make_async_remote_copy(
@@ -208,13 +229,34 @@
             @pl.when(inside(offset))
             def _():
                 fn(offset)
+
+    def when_sent(fn):
+        for offset in offsets:
+            own_part = inside(offset)
+            if offset == 2:
+                own_part = own_part & (odd == 0)
+            elif offset == -2:
+                own_part = own_part & (odd == 1)
+
+            @pl.when(own_part)
+            def _():
+                fn(offset)
+
+    def when_relay(fn):
+        @pl.when((odd == 0) & inside(-1))
+        def _():
+            fn(-1)
+
+        @pl.when((odd == 1) & inside(1))
+        def _():
+            fn(1)
 
     def operate(first):
         for c in range(cl_dev):
             value = direction[c]
             window[REACH, c] = value.astype(jnp.bfloat16)
             turned[c] = value.T.astype(jnp.bfloat16)
-        when_inside(lambda o: window_copy(o).start())
+        when_sent(lambda o: window_copy(o).start())
 
         if first:
             loads[0].wait()
@@ -252,26 +294,60 @@
 
         times(cl_dev * near_cl, mirror)
 
-        for o in [1, -1, 2, -2, 0]:
+        def relay(side):
+            window_from(side).wait_recv()
+            window_relay(side).start()
+
+        when_relay(relay)
+
+        def gather(o, target, kind=None, extra=None):
             for c in range(cl_dev):
                 hits = [
                     jnp.where((offset_ref[i] == o) & (column_ref[i] == c), 1.0, 0.0).astype(jnp.float32)
                     for i in range(cl_dev * near_cl)
                 ]
-                target = image.at[c] if o == 0 else returned.at[o + REACH, c]
-
-                def fold(t):
+
+                def fold(t, top):
                     rows = pl.ds(pl.multiple_of(t * 64, 64), 64)
                     total = mirrored[0, rows] * hits[0]
                     for i in range(1, cl_dev * near_cl):
                         total = total + mirrored[i, rows] * hits[i]
-                    target[rows] = total
-
-                times(panels // 64, fold)
-            if o:
-                @pl.when(inside(o))
-                def _():
-                    mirror_copy(o).start()
+                    if extra is not None:
+                        total = total + extra[c, rows]
+                    target[c, rows] = total
+                    return jnp.maximum(top, jnp.max(jnp.abs(total).reshape(8, 8, modes), axis=0))
+
+                top = lax.fori_loop(0, panels // 64, fold, jnp.zeros((8, modes), jnp.float32))
+                if kind is not None:
+                    top = jnp.maximum(jnp.max(top, axis=0, keepdims=True), 1e-30)
+                    scale_out[kind, c] = jnp.broadcast_to(top * (1.0 / STEPS), (8, modes))
+                    finer = STEPS / top
+
+                    def code(t):
+                        rows = pl.ds(pl.multiple_of(t * 64, 64), 64)
+                        value = jnp.floor(target[c, rows] * finer + 0.5)
+                        returned[kind, c, rows] = value.astype(jnp.int32).astype(jnp.int16)
+
+                    times(panels // 64, code)
+
+        gather(-across, partial)
+        partial_copy().start()
+        gather(across, stage, 1)
+
+        @pl.when(inside(across))
+        def _():
+            post_mirror(1)
+
+        gather(beside, stage, 0)
+        post_mirror(0)
+        partial_copy().wait_recv()
+        gather(joint, stage, 2, partner)
+
+        @pl.when(inside(joint))
+        def _():
+            post_mirror(2)
+
+        gather(0, image)
 
         if first:
             loads[2].wait()
@@ -279,7 +355,17 @@
             both = fast_dot(own[c], window[REACH, c]) + fast_dot(turned[c], own[c]).T
             image[c] += 0.5 * both + diag_ref[c] * direction[c]
 
-        when_inside(lambda o: window_from(o).wait_recv())
+        for side in (-1, 1):
+            taken = (odd == 0) if side < 0 else (odd == 1)
+
+            @pl.when(inside(side) & jnp.logical_not(taken))
+            def _():
+                window_from(side).wait_recv()
+
+            @pl.when(inside(2 * side))
+            def _():
+                window_from(2 * side).wait_recv()
+
 
         def forward(i):
             c, q = i // near_cl, i % near_cl
@@ -305,15 +391,22 @@
 
         times(cl_dev * tiles, expand)
 
-        def collect(o):
-            mirror_from(o).wait_recv()
-            image[...] += landed[REACH + o]
-
-        when_inside(collect)
-
-    def settle():
-        when_inside(lambda o: window_copy(o).wait_send())
-        when_inside(lambda o: mirror_copy(o).wait_send())
+        def collect(kind):
+            mirror_copy(kind).wait_recv()
+            scale_copy(kind).wait_recv()
+            for c in range(cl_dev):
+                value = landed[kind, c].astype(jnp.int32).astype(jnp.float32)
+                image[c] += value * scale_in[kind, c, 0:1]
+
+        collect(0)
+        pl.when(inside(-across))(lambda: collect(1))
+        pl.when(inside(joint))(lambda: collect(2))
+        when_sent(lambda o: window_copy(o).wait_send())
+        when_relay(lambda side: window_relay(side).wait_send())
+        partial_copy().wait_send()
+        sent_mirror(0)
+        pl.when(inside(across))(lambda: sent_mirror(1))
+        pl.when(inside(joint))(lambda: sent_mirror(2))
         times(devices - 1, lambda k: far_copy(k + 1, lax.rem(me + k + 1, devices), me).wait_send())
 
     def flat(ref):
@@ -339,7 +432,6 @@
     field_ref[...] = combine(direction, step)
     resid_ref[...] = resid_ref[...] - combine(image, step)
     direction[...] = resid_ref[...] + combine(direction, blend)
-    settle()
 
     operate(False)
     part_b[...] = gram(direction, image).reshape(part_b.shape)
@@ -348,7 +440,6 @@
     step = hdot(inv_curv, later)
     field_ref[...] = field_ref[...] + combine(direction, step)
     resid_ref[...] = resid_ref[...] - combine(image, step)
-    settle()
 
 
 def shards(
@@ -391,9 +482,14 @@
             pltpu.VMEM((span,) + block, bf16),
             dma((2, span)),
             pltpu.VMEM((cl_dev * near_cl, panels, modes), f32),
-            pltpu.VMEM((span,) + block, f32),
-            pltpu.VMEM((span,) + block, f32),
-            dma((2, span)),
+            pltpu.VMEM((3,) + block, jnp.int16),
+            pltpu.VMEM((3,) + block, jnp.int16),
+            pltpu.VMEM((3, cl_dev, 8, modes), f32),
+            pltpu.VMEM((3, cl_dev, 8, modes), f32),
+            pltpu.VMEM(block, f32),
+            pltpu.VMEM(block, f32),
+            pltpu.VMEM(block, f32),
+            dma((2, 7)),
             pltpu.VMEM((far_dev + 1,) + half, bf16),
             pltpu.VMEM((devices, capacity) + half, bf16),
             pltpu.VMEM((devices, capacity) + half, bf16),

time: 197 us -> 141 us (0.72)
  Pallas kernels: 186 us -> 131 us
    pallas_call x1, Pallas kernels: 186 us -> 131 us  [shards(): pl.pallas_call(functools.partial(kernel, devices), out_shape=[jax.ShapeDt...]
where the time goes in v2:
time: 141 us
  Pallas kernels  131 us (93%)
  local copies, waits for them, and re-layouts  6.7 us (5%)
  other arithmetic  2.51 us (2%)
    pallas_call x1, Pallas kernels, shards(): pl.pallas_call(functools.partial(kernel, devices), out_shape=[jax.ShapeDt...  131 us
    unnamed x12, local copies, waits for them, and re-layouts  5.82 us

profile of v2, /device:TPU:0, one launch (start us, length us, event | category | flops | bytes accessed | tf_op | source)
XLA Modules:
  0.0 140.7 jit_solution(7579471023033128200)
XLA Ops:
  0.6 0.7 fusion
  1.4 0.2 reduce_window_sum.11
  1.5 0.8 select_reduce_fusion.1.rank_ref
  2.4 0.7 iota_add_fusion
  3.0 0.1 select_reduce_fusion
  3.2 0.9 broadcast_in_dim.14.diag_ref
  4.1 0.0 copy-start
  4.1 0.6 copy-done
  4.7 0.0 copy-start.1
  4.7 1.2 copy-done.1
  5.9 0.0 copy-start.2
  5.9 1.0 copy-done.2
  7.0 0.0 copy-start.3
  7.0 0.7 copy-done.3
  7.6 0.0 copy-start.4
  7.6 0.7 copy-done.4
  8.3 130.9 %shard_map.95 = (f32[2,512,128]{2,1,0:T(8,128)S(1)}, f32[2,512,128]{2,1,0:T(8,128)S(1)}) custom-call(f32[2,512,128]{2,1,0:T(8,128)S(1)} %copy-done.2, f32[2,512,128]{2,1,0:T(8,128)S(1)} %broadcast_in_dim.14.diag_ref, bf16[2,512,512]{2,1,0:T(8,128)(2,1)S(1)} %copy-done.1, bf16[2,512,2048]{2,1,0:T(8,128)(2,1)} %near_hbm.1, bf16[2,512,2048]{2,1,0:T(8,128)(2,1)} %far_hbm.1, ...), custom_call_target="tpu_custom_call" | custom-call | flops 9663676416 | bytes 12582912 | tf_op jit(solution)/shard_map/pallas_call | solution.py:470
  139.2 0.8 copy.12
  140.0 0.8 copy.13
  (1 shorter events, 0.0 us)
Async XLA Ops:
  4.1 0.7 copy-start
  4.7 1.2 copy-start.1
  5.9 1.0 copy-start.2
  7.0 0.7 copy-start.3
  7.6 0.7 copy-start.4
